TPU v7x, 256 devices: a whole 4x4x8 slice. The times are simulated.
256 devices in a mesh: dp: 4 (over y_hi, core), ctx: 64 (over x, z, y_lo).
Axes of the slice: x: 4, y: 4 (y_hi: 2, y_lo: 2; y = y_hi * 2 + y_lo), z: 8, core: 2. Of those that a mesh axis runs over, the one named last changes fastest.
Arguments:
- queries: bfloat16 [32768, 1536], P(('dp', 'ctx')), parts along dimension 0, may hold values from -23 to 23
- keys: bfloat16 [32768, 128], P(('dp', 'ctx')), parts along dimension 0, may hold values from -6 to 6
- values: bfloat16 [32768, 128], P(('dp', 'ctx')), parts along dimension 0, may hold values from -6 to 6
- forward_out: bfloat16 [32768, 1536], P(('dp', 'ctx')), parts along dimension 0, may hold values from -6 to 6
- out_grad: bfloat16 [32768, 1536], P(('dp', 'ctx')), parts along dimension 0, may hold values from -24 to 24
- span_ids: int32 [512], P(('dp', 'ctx')), parts along dimension 0, may hold values from 0 to 127, as said below
Outputs:
- d_queries: bfloat16 [32768, 1536], P(('dp', 'ctx')), parts along dimension 0
- d_keys: float32 [32768, 128], P(('dp', 'ctx')), parts along dimension 0
- d_values: float32 [32768, 128], P(('dp', 'ctx')), parts along dimension 0
There are 4 independent parts, one for each index of `dp`. A program takes and returns all parts, laid end to end along the dimension named above; each array names one. Nothing has to cross between parts.
Inputs may be any that keep to these rules, and one draw needn't show every extreme that they name: `span_ids`: each span number appears once, and the two entries of one device sum to 127.
All inputs are finite; a program needn't handle non-finite values.
Results may differ from a plain program's by a relative error of at most 0.0047.
Values may be sent and summed in bfloat16 or wider, within the bound.
No kernel may reach another device: no remote copies, remote signals or barrier semaphores. Data moves between devices by JAX's collectives and lax.ppermute only.
A program may use at most 64 MiB of HBM per device.

v0:
```python
import functools
import math

import jax
import jax.numpy as jnp
from jax import lax
from jax.experimental import pallas as pl
from jax.experimental.pallas import tpu as pltpu
from jax.sharding import PartitionSpec as P

NX, NZ, NY = 4, 8, 2
DEVICES = NX * NZ * NY
SPAN = 64
SPANS = 2 * DEVICES
WIDTH = 128
HEADS = 12
ROWS = HEADS * SPAN
KINDS = 2 * NY
COLS = KINDS * ROWS
KEYS = SPANS // NY * SPAN
STATS_TILE = 8 * SPAN
TILE = 8 * SPAN
BLOCK = 2 * SPAN + 16
FACTOR = 1.0 / math.sqrt(WIDTH)
SCALE = FACTOR * math.log2(math.e)
NEG = -1e30
SAFE = 64.0
VMEM_LIMIT = 28 * 1024 * 1024

F32 = jnp.float32
BF16 = jnp.bfloat16


def place(x, z, y):
    return ((x % NX) * NZ + z % NZ) * NY + y % NY


def shift(block, dx=0, dz=0, dy=0):
    pairs = [
        (place(x, z, y), place(x + dx, z + dz, y + dy))
        for x in range(NX)
        for z in range(NZ)
        for y in range(NY)
    ]
    return lax.ppermute(block, "ctx", pairs)


def spans_of(meta):
    return meta[0], SPANS - 1 - meta[0], meta[1], SPANS - 1 - meta[1]


def pick(spans, kind):
    result = spans[0]
    for i in range(1, KINDS):
        result = jnp.where(kind == i, spans[i], result)
    return result


def columns(start, width=ROWS):
    return pl.ds(pl.multiple_of(start, WIDTH), width)


def numbers_rows(first, second):
    index = lax.broadcasted_iota(jnp.int32, (16, 2 * WIDTH), 0)
    return jnp.where(index < 8, first, second).astype(F32).astype(BF16)


def pack_kernel(ids, where, keys_any, values_any, kept, sent, keys, values, sem, sem_v):
    copies = [
        pltpu.make_async_copy(keys_any, keys, sem),
        pltpu.make_async_copy(values_any, values, sem_v),
    ]
    for copy in copies:
        copy.start()
    for copy in copies:
        copy.wait()
    keep = jnp.where((ids[0] & 1) == where[2], 0, 1)
    for target, slot in ((kept, keep), (sent, 1 - keep)):
        rows = pl.ds(pl.multiple_of(slot * SPAN, SPAN), SPAN)
        target[:SPAN, :WIDTH] = keys[rows, :]
        target[:SPAN, WIDTH:] = values[rows, :]
        number = jnp.where(slot == 0, ids[0], ids[1])
        target[SPAN:, :] = numbers_rows(number, ids[0])


def join_kernel(ids, where, kept, given, block, meta):
    block[:SPAN, :] = kept[:SPAN, :]
    block[SPAN : 2 * SPAN, :] = given[:SPAN, :]
    mine, other = kept[SPAN:, :].astype(F32), given[SPAN:, :].astype(F32)
    block[2 * SPAN :, :] = jnp.concatenate([mine[:8], other[:8]], axis=0).astype(BF16)
    meta[0] = ids[0]
    meta[1] = other[8, 0].astype(jnp.int32)
    for i in range(3):
        meta[2 + i] = where[i]


def place_heads(own, refs, sources):
    for slot in range(2):
        rows = slice(slot * SPAN, (slot + 1) * SPAN)
        for b in range(HEADS // 2):
            lanes = [slice(h * WIDTH, (h + 1) * WIDTH) for h in (2 * b, 2 * b + 1)]
            start = ((0 if own else 2) + slot) * ROWS + b * WIDTH
            target = slice(start, start + WIDTH)
            blocks = []
            for source in sources:
                blocks.append(jnp.concatenate([source[rows, i] for i in lanes], axis=0))
            for (tall, wide), block in zip(refs, blocks):
                wide[target, :] = block
                tall[:, target] = block.T
            if own:
                yield target, blocks


def own_rows_kernel(q_own, g_own, o_own, qs, gs, qt, gt, delta):
    for target, (_, g, o) in place_heads(True, ((qt, qs), (gt, gs)), (q_own, g_own, o_own)):
        total = jnp.sum((g.astype(F32) * o.astype(F32)).T, axis=0, keepdims=True)
        delta[:, target] = jnp.broadcast_to(total, (8, WIDTH))


def other_rows_kernel(rows, _wide, _tall, wide, tall):
    for _ in place_heads(False, ((tall, wide),), (rows,)):
        pass


def plane_kernel(*refs):
    pieces, plane = refs[:-1], refs[-1]
    index = lax.broadcasted_iota(jnp.int32, (16, 2 * WIDTH), 0)
    numbers = jnp.zeros((16, 2 * WIDTH), F32)
    count = 0
    for piece in pieces:
        for b in range(piece.shape[0] // BLOCK):
            start = b * BLOCK
            plane[count * SPAN : (count + 2) * SPAN, :] = piece[start : start + 2 * SPAN, :]
            tail = piece[start + 2 * SPAN : start + BLOCK, :].astype(F32)
            numbers = jnp.where(index == count, tail[0:1], numbers)
            numbers = jnp.where(index == count + 1, tail[8:9], numbers)
            count += 2
    plane[count * SPAN :, :] = numbers.astype(BF16)


def read_numbers(parts):
    found = []
    for part in parts:
        tail = part[2 * NZ * SPAN :, :WIDTH].astype(F32)
        for i in range(2 * NZ):
            found.append((tail[i, 0].astype(jnp.int32), part, i * SPAN))
    return found


def sort_kernel(n_parts, *refs):
    parts, (pairs, sums, dqt) = refs[:n_parts], refs[n_parts:]
    sums[...] = jnp.zeros(sums.shape, F32)
    dqt[...] = jnp.zeros(dqt.shape, F32)
    for number, part, row in read_numbers(parts):
        target = pl.multiple_of(number // NY * SPAN, SPAN)
        pairs[pl.ds(target, SPAN), :] = part[row : row + SPAN, :]


def hide(scores, offsets):
    shape = (scores.shape[0], WIDTH)
    index = lax.broadcasted_iota(jnp.int32, shape, 0)
    offset = jnp.full(shape, offsets[0], jnp.int32)
    for i in range(1, len(offsets)):
        offset = jnp.where(index >= i * SPAN, offsets[i], offset)
    row = lax.broadcasted_iota(jnp.int32, shape, 1) & (SPAN - 1)
    lowered = jnp.where(offset * SPAN + (index & (SPAN - 1)) > row, 2 * NEG, 0.0)
    return scores + jnp.concatenate([lowered] * (scores.shape[1] // WIDTH), axis=1)


def statistics_kernel(n_parts, first, last, meta, *refs):
    parts, refs = refs[:n_parts], list(refs[n_parts:])
    qt = refs.pop(0)
    before_ref = None if first else refs.pop(0)
    delta = refs.pop(0) if last else None
    out, row_max, row_sum, base, top, extra, keys, ordered = refs
    spans = spans_of(meta)
    found = read_numbers(parts)
    for number, part, row in found:
        rank = sum((other < number).astype(jnp.int32) for other, _, _ in found)
        ordered[rank] = number
        target = pl.multiple_of(rank * SPAN, SPAN)
        keys[pl.ds(target, SPAN), :] = part[row : row + SPAN, :WIDTH]
    if first:
        row_max[...] = jnp.full((8, COLS), NEG, F32)
        row_sum[...] = jnp.zeros((8, COLS), F32)
    else:
        row_max[...] = before_ref[:8, :]
        row_sum[...] = before_ref[8:, :]
    group = STATS_TILE // SPAN

    def visit_all(visit, width, always_masked):
        def step(i, carry):
            kind = i // (ROWS // width)
            span = pick(spans, kind)
            cols = columns(i * width, width)

            def scores(tile, masked):
                k = keys[pl.ds(pl.multiple_of(tile * STATS_TILE, STATS_TILE), STATS_TILE), :]
                s = jnp.dot(k, qt[:, cols], preferred_element_type=F32) * SCALE
                if masked:
                    offsets = [ordered[tile * group + i] - span for i in range(group)]
                    s = hide(s, offsets)
                visit(s.reshape(STATS_TILE // 8, 8, width), cols)

            full = sum((number < span).astype(jnp.int32) for number, _, _ in found) // group
            seen = sum((number <= span).astype(jnp.int32) for number, _, _ in found)
            if always_masked:
                tiles = (seen + group - 1) // group
                lax.fori_loop(0, tiles, lambda t, c: scores(t, True), None)
                return carry
            lax.fori_loop(0, full, lambda t, c: scores(t, False), None)

            @pl.when(seen > full * group)
            def _():
                scores(full, True)

            return carry

        lax.fori_loop(0, COLS // width, step, 0)

    def against_base(s, cols):
        top[:, cols] = jnp.maximum(top[:, cols], jnp.max(s, axis=0))
        extra[:, cols] += jnp.sum(jnp.exp2(s - base[:, cols][None]), axis=0)

    def against_maximum(s, cols):
        before = row_max[:, cols]
        after = jnp.maximum(before, jnp.max(s, axis=0))
        fresh = jnp.sum(jnp.exp2(s - after[None]), axis=0)
        row_sum[:, cols] = row_sum[:, cols] * jnp.exp2(before - after) + fresh
        row_max[:, cols] = after

    unset = row_max[...] <= NEG
    base[...] = jnp.where(unset, 0.0, row_max[...])
    top[...] = jnp.full((8, COLS), 2 * NEG, F32)
    extra[...] = jnp.zeros((8, COLS), F32)
    visit_all(against_base, ROWS, False)
    unset = row_max[...] <= NEG
    seen = top[...] > NEG
    gap = top[...] - base[...]
    far = seen & ((gap > SAFE) | (unset & (gap < -SAFE)))
    any_far = jnp.max(jnp.where(far, 1.0, 0.0)) > 0.0

    @pl.when(jnp.logical_not(any_far))
    def _():
        empty = unset & jnp.logical_not(seen)
        after = jnp.maximum(base[...], top[...])
        total = (row_sum[...] + extra[...]) * jnp.exp2(base[...] - after)
        row_sum[...] = jnp.where(empty, 0.0, total)
        row_max[...] = jnp.where(empty, NEG, after)

    @pl.when(any_far)
    def _():
        visit_all(against_maximum, WIDTH, True)

    if not last:
        out[:8, :] = row_max[...]
        out[8:, :] = row_sum[...]
    else:
        most = jnp.max(row_max[...], axis=0, keepdims=True)
        total = jnp.sum(row_sum[...] * jnp.exp2(row_max[...] - most), axis=0, keepdims=True)
        out[0:1, :] = most
        out[1:2, :] = total
        out[2:3, : 2 * ROWS] = delta[0:1, :]
        out[2:3, 2 * ROWS :] = jnp.zeros((1, 2 * ROWS), F32)
        out[3:8, :] = jnp.zeros((5, COLS), F32)


ORDER = (2, 1, NX - 1, 0)
TILES = KEYS // NX // TILE
STAGES = ((0,), (1, 2), (3,))


Z_ORDER = (0, 4, 1, 7, 5, 2, 3, 6)


def gradients_kernel(stage, meta, pairs, qs, gs, qt, gt, mine_ref, other_ref, _sums, _dqt, *refs):
    sums, dqt = refs[:2]
    outs, (level, delta) = refs[2:-2], refs[-2:]
    spans = spans_of(meta)
    my_x, my_z, parity = meta[2], meta[3], meta[4]
    half = 2 * ROWS
    for mine, other in ((slice(0, half), slice(half, COLS)), (slice(half, COLS), slice(0, half))):
        top = jnp.maximum(mine_ref[0:1, mine], other_ref[0:1, other])
        total = mine_ref[1:2, mine] * jnp.exp2(mine_ref[0:1, mine] - top)
        total += other_ref[1:2, other] * jnp.exp2(other_ref[0:1, other] - top)
        level[:, mine] = top + jnp.log2(total)
        delta[:, mine] = mine_ref[2:3, mine] + other_ref[2:3, other]
    group = TILE // SPAN
    lasts = [jnp.maximum(span - parity, 0) // NY // group for span in spans]
    firsts = [(my_x + off) % NX * TILES for off in ORDER]
    counts = [
        sum(jnp.clip(last - first + 1, 0, TILES) for last in lasts) for first in firsts
    ]
    ready = [sum(counts[: entries[-1] + 1]) for entries in STAGES]
    everything = ready[-1]
    ends = [
        jnp.maximum(needed, (everything * (i + 1) + len(STAGES) - 1) // len(STAGES))
        for i, needed in enumerate(ready)
    ]
    begin = 0 if stage == 0 else ends[stage - 1]
    end = ends[stage]

    def visit(kind, tile, masked):
        span = pick(spans, kind)
        cols = columns(kind * ROWS)
        rows = pl.ds(pl.multiple_of(tile * TILE, TILE), TILE)
        k = pairs[rows, :WIDTH]
        v = pairs[rows, WIDTH:]
        s = jnp.dot(k, qt[:, cols], preferred_element_type=F32) * SCALE
        if masked:
            s = hide(s, [(tile * group + j) * NY + parity - span for j in range(group)])
        p = jnp.exp2(s - level[:, cols])
        dp = jnp.dot(v, gt[:, cols], preferred_element_type=F32)
        ds = (p * (dp - delta[:, cols])).astype(BF16)
        d_value = jnp.dot(p.astype(BF16), gs[cols, :], preferred_element_type=F32)
        d_key = jnp.dot(ds, qs[cols, :], preferred_element_type=F32)
        dqt[:, cols] += jnp.dot(k.T, ds, preferred_element_type=F32)
        sums[rows, :WIDTH] += d_key
        sums[rows, WIDTH:] += d_value

    def step(i, done):
        entry, kind = i // KINDS, i % KINDS
        first, last = pick(firsts, entry), pick(lasts, kind)
        count = jnp.clip(last - first + 1, 0, TILES)

        def part_step(part, carry):
            tile = first + part

            @pl.when(tile < last)
            def _():
                visit(kind, tile, False)

            @pl.when(tile == last)
            def _():
                visit(kind, tile, True)

            return carry

        low, high = jnp.clip(begin - done, 0, count), jnp.clip(end - done, 0, count)
        lax.fori_loop(low, high, part_step, 0)
        return done + count

    lax.fori_loop(0, len(ORDER) * KINDS, step, jnp.int32(0))
    pair = 2 * SPAN
    for entry, out in zip(STAGES[stage], outs):
        for i, z_off in enumerate(Z_ORDER):
            start = firsts[entry] * TILE + (my_z + z_off) % NZ * pair
            source = pl.ds(pl.multiple_of(start, pair), pair)
            out[i * pair : (i + 1) * pair, :] = sums[source, :].astype(out.dtype)


def d_queries_kernel(dqt, dq_own, dq_other):
    for device, out in enumerate((dq_own, dq_other)):
        for slot in range(2):
            for b in range(ROWS // WIDTH):
                start = (2 * device + slot) * ROWS + b * WIDTH
                block = dqt[:, start : start + WIDTH].T * FACTOR
                for half in range(2):
                    h = 2 * b + half
                    out[slot * SPAN : (slot + 1) * SPAN, h * WIDTH : (h + 1) * WIDTH] = block[
                        half * SPAN : (half + 1) * SPAN
                    ].astype(out.dtype)


def run(kernel, scalars, arrays, outs, scratch, flops, name, far=(), aliases=None, scalar_outs=()):
    spaces = [pltpu.SMEM] * len(scalars)
    spaces += [pltpu.HBM if i in far else pltpu.VMEM for i in range(len(arrays))]
    return pl.pallas_call(
        kernel,
        out_shape=[jax.ShapeDtypeStruct(s, d) for s, d in outs],
        in_specs=[pl.BlockSpec(memory_space=space) for space in spaces],
        out_specs=[
            pl.BlockSpec(memory_space=pltpu.SMEM if i in scalar_outs else pltpu.VMEM)
            for i in range(len(outs))
        ],
        scratch_shapes=scratch,
        input_output_aliases=aliases or {},
        compiler_params=pltpu.CompilerParams(vmem_limit_bytes=VMEM_LIMIT),
        cost_estimate=pl.CostEstimate(flops=flops, bytes_accessed=10**5, transcendentals=0),
        name=name,
    )(*scalars, *arrays)


WIDE = ((COLS, WIDTH), BF16)
TALL = ((WIDTH, COLS), BF16)
FLAT = ((8, COLS), F32)
OWN = (2 * SPAN, HEADS * WIDTH)
SUMS = ((KEYS, 2 * WIDTH), F32)
DQT = ((WIDTH, COLS), F32)


def statistics(meta, parts, qt, before, delta):
    first, last = before is None, delta is not None
    count = 2 * NZ * len(parts)
    arrays = list(parts) + [qt] + [a for a in (before, delta) if a is not None]
    return run(
        functools.partial(statistics_kernel, len(parts), first, last),
        [meta],
        arrays,
        [FLAT if last else ((16, COLS), F32)],
        [pltpu.VMEM((8, COLS), F32)] * 5
        + [pltpu.VMEM((count * SPAN, WIDTH), BF16), pltpu.SMEM((count,), jnp.int32)],
        2 * 10**9,
        "row_statistics",
    )[0]


def other_rows(rows, wide, tall):
    return run(
        other_rows_kernel, [], [rows, wide, tall], [WIDE, TALL], [], 10**9, "other_rows",
        aliases={1: 0, 2: 1},
    )


def gradients(stage, meta, arrays, state, dtype):
    share = ((KEYS // NX, 2 * WIDTH), dtype)
    count = 1 + len(arrays)
    return run(
        functools.partial(gradients_kernel, stage),
        [meta],
        arrays + list(state),
        [SUMS, DQT] + [share] * len(STAGES[stage]),
        [pltpu.VMEM((1, COLS), F32)] * 2,
        8 * 10**9,
        "gradients",
        aliases={count: 0, count + 1: 1},
    )


def per_device(queries, keys, values, forward_out, out_grad, span_ids):
    me = lax.axis_index("ctx")
    my_x, my_z, my_y = me // (NZ * NY), (me // NY) % NZ, me % NY
    where = jnp.stack([my_x, my_z, my_y]).astype(jnp.int32)
    carried = ((SPAN + 16, 2 * WIDTH), BF16)
    sem = pltpu.SemaphoreType.DMA
    local = pltpu.VMEM((2 * SPAN, WIDTH), BF16)
    kept, sent = run(
        pack_kernel, [span_ids, where], [keys, values], [carried] * 2, [local, local, sem, sem],
        10, "pack", far=(0, 1),
    )
    given = shift(sent, dy=1)
    block, meta = run(
        join_kernel, [span_ids, where], [kept, given],
        [((BLOCK, 2 * WIDTH), BF16), ((5,), jnp.int32)], [], 10, "join", scalar_outs=(1,),
    )

    block, queries, out_grad, forward_out = lax.optimization_barrier(
        (block, queries, out_grad, forward_out)
    )
    q_other = shift(queries, dy=1)
    g_other = shift(out_grad, dy=1)
    qs, gs, qt, gt, delta = run(
        own_rows_kernel, [], [queries, out_grad, forward_out],
        [WIDE, WIDE, TALL, TALL, ((8, COLS // 2), F32)], [], 10**9, "own_rows",
    )
    below, above, across = shift(block, dz=1), shift(block, dz=-1), shift(block, dz=NZ // 2)
    below, above, across, qs, gs, qt, gt, delta = lax.optimization_barrier(
        (below, above, across, qs, gs, qt, gt, delta)
    )
    further = [
        shift(jnp.concatenate([across, below], axis=0), dz=1),
        shift(jnp.concatenate([across, above], axis=0), dz=-1),
    ]
    (plane,) = run(
        plane_kernel, [], [block, across, below, above] + further,
        [((2 * NZ * SPAN + 16, 2 * WIDTH), BF16)], [], 10, "plane",
    )
    qs, qt = other_rows(q_other, qs, qt)
    gs, gt = other_rows(g_other, gs, gt)
    near, far, back = (shift(plane, dx=d) for d in range(1, NX))
    gathered = [plane, near, back, far]
    stats = None
    for i, part in enumerate(gathered):
        last = i == len(gathered) - 1
        stats = statistics(meta, [part], qt, stats, delta if last else None)
    other_stats = shift(stats, dy=1)
    pairs, *state = run(
        functools.partial(sort_kernel, len(gathered)), [], gathered,
        [((KEYS, 2 * WIDTH), BF16), SUMS, DQT], [], 10**9, "sort",
    )

    arrays = [pairs, qs, gs, qt, gt, stats, other_stats]
    *state, far = gradients(0, meta, arrays, state, BF16)
    far = shift(far, dx=ORDER[0])
    *state, up, down = gradients(1, meta, arrays, state, BF16)
    up, down = shift(up, dx=1), shift(down, dx=-1)
    far, *state = lax.optimization_barrier((far, *state))
    *state, own = gradients(2, meta, arrays, state, F32)
    dqt = state[1]
    over_x = [own, far, up, down]
    dq_own, dq_sent = run(
        d_queries_kernel, [], [dqt], [(OWN, F32), (OWN, BF16)], [], 10**8, "d_queries"
    )

    over_x = sum(part.astype(F32) for part in over_x)
    over_x, dq_own, dq_sent = lax.optimization_barrier((over_x, dq_own, dq_sent))
    pair = 2 * SPAN
    mine, across, above, below, up, down = (
        over_x[a * pair : b * pair] for a, b in ((0, 1), (1, 2), (2, 3), (3, 4), (4, 6), (6, 8))
    )
    from_below = shift(up.astype(BF16), dz=1).astype(F32)
    from_above = shift(down.astype(BF16), dz=-1).astype(F32)
    across = across + from_below[:pair] + from_above[:pair]
    above = above + from_below[pair:]
    below = below + from_above[pair:]
    over_z = mine
    for part, d in ((across, NZ // 2), (above, 1), (below, -1)):
        over_z = over_z + shift(part.astype(BF16), dz=d).astype(F32)
    dq_given = shift(dq_sent, dy=1)
    over_z, dq_given = lax.optimization_barrier((over_z, dq_given))
    d_queries = (dq_own + dq_given.astype(F32)).astype(BF16)
    first = my_y == 0
    upper, lower = over_z[:SPAN], over_z[SPAN:]
    given = shift(jnp.where(first, lower, upper), dy=1)
    final = jnp.where(
        first,
        jnp.concatenate([upper, given], axis=0),
        jnp.concatenate([given, lower], axis=0),
    )
    return (d_queries, final[:, :WIDTH] * FACTOR, final[:, WIDTH:])


def solution(mesh):
    rows = P(("dp", "ctx"), None)
    return jax.shard_map(
        per_device,
        mesh=mesh,
        in_specs=(rows, rows, rows, rows, rows, P(("dp", "ctx"))),
        out_specs=(rows, rows, rows),
        check_vma=False,
    )
```

profile of v0, /device:TPU:8, one launch (start us, length us, event | category | flops | bytes accessed | tf_op | source)
XLA Modules:
  0.0 146.2 jit_solution(1193202934550628910)
XLA Ops:
  0.7 0.1 pad_add_fusion.where
  0.7 0.8 copy-done
  1.5 0.8 copy-done.1
  2.3 0.7 copy-done.2
  2.9 0.7 pack.1
  3.6 2.3 %collective-permute-start = (bf16[80,256]{1,0:T(8,128)(2,1)S(1)}, bf16[80,256]{1,0:T(8,128)(2,1)S(1)}, u32[]{:S(2)}, u32[]{:S(2)}) collective-permute-start(bf16[80,256]{1,0:T(8,128)(2,1)S(1)} %get-tuple-element.51), channel_id=1, source_target_pairs={{0,1},{1,0},{2,3},{3,2},{4,5},{5,4},{6,7},{7,6},{8,9},{9,8},{10,11... | collective-permute-start | bytes 122888 | tf_op jit(solution)/shard_map/ppermute | solution.py:45
  5.9 2.0 %collective-permute-done.given = bf16[80,256]{1,0:T(8,128)(2,1)S(1)} collective-permute-done((bf16[80,256]{1,0:T(8,128)(2,1)S(1)}, bf16[80,256]{1,0:T(8,128)(2,1)S(1)}, u32[]{:S(2)}, u32[]{:S(2)}) %collective-permute-start) | collective-permute-done | bytes 40992 | tf_op jit(solution)/shard_map/ppermute | solution.py:45
  7.8 1.2 join.1
  9.0 7.1 %collective-permute-start.3 = (bf16[144,256]{1,0:T(8,128)(2,1)S(1)}, bf16[144,256]{1,0:T(8,128)(2,1)S(1)}, u32[]{:S(2)}, u32[]{:S(2)}) collective-permute-start(bf16[144,256]{1,0:T(8,128)(2,1)S(1)} %get-tuple-element.54.refs_0_), channel_id=1, source_target_pairs={{0,8},{1,9},{2,10},{3,11},{4,12},{5,13},{6,14},{7,15},{8,0},{9,1},... | collective-permute-start | bytes 221192 | tf_op jit(solution)/shard_map/ppermute | solution.py:45
  16.1 0.1 collective-permute-start.2
  16.3 1.9 %collective-permute-start.1 = (bf16[144,256]{1,0:T(8,128)(2,1)S(1)}, bf16[144,256]{1,0:T(8,128)(2,1)S(1)}, u32[]{:S(2)}, u32[]{:S(2)}) collective-permute-start(bf16[144,256]{1,0:T(8,128)(2,1)S(1)} %get-tuple-element.54.refs_0_), channel_id=1, source_target_pairs={{0,2},{1,3},{2,4},{3,5},{4,6},{5,7},{6,8},{7,9},{8,10},{9,11},{10,... | collective-permute-start | bytes 221192 | tf_op jit(solution)/shard_map/ppermute | solution.py:45
  18.2 1.0 copy-done.3
  19.2 1.0 copy-done.4
  20.2 1.5 %own_rows.1 = (bf16[3072,128]{1,0:T(8,128)(2,1)S(1)}, bf16[3072,128]{1,0:T(8,128)(2,1)S(1)}, bf16[128,3072]{1,0:T(8,128)(2,1)S(1)}, bf16[128,3072]{1,0:T(8,128)(2,1)S(1)}, f32[8,1536]{1,0:T(8,128)S(1)}) custom-call(bf16[128,1536]{1,0:T(8,128)(2,1)S(1)} %copy-done.4, bf16[128,1536]{1,0:T(8,128)(2,1)} %g_own, bf16[128,1536]{1,0:T(8,128)(2,1)S(1)} %copy-done.3), custom_call_target="tpu_custom_call" | custom-call | flops 1000000000 | bytes 100000 | tf_op jit(solution)/shard_map/own_rows/pallas_call | solution.py:368
  21.7 0.0 collective-permute-done.3.refs_1_
  21.7 0.1 collective-permute-done.1.refs_2_
  21.8 1.7 %collective-permute-start.5 = (bf16[288,256]{1,0:T(8,128)(2,1)S(1)}, bf16[288,256]{1,0:T(8,128)(2,1)S(1)}, u32[]{:S(2)}, u32[]{:S(2)}) collective-permute-start(bf16[288,256]{1,0:T(8,128)(2,1)S(1)} %get-tuple-element.107), channel_id=1, source_target_pairs={{0,14},{1,15},{2,0},{3,1},{4,2},{5,3},{6,4},{7,5},{8,6},{9,7},{10,... | collective-permute-start | bytes 442376 | tf_op jit(solution)/shard_map/ppermute | solution.py:45
  23.5 0.4 collective-permute-start.4
  23.9 0.4 collective-permute-start.9
  24.4 2.7 %collective-permute-done.5.refs_5_ = bf16[288,256]{1,0:T(8,128)(2,1)S(1)} collective-permute-done((bf16[288,256]{1,0:T(8,128)(2,1)S(1)}, bf16[288,256]{1,0:T(8,128)(2,1)S(1)}, u32[]{:S(2)}, u32[]{:S(2)}) %collective-permute-start.5) | collective-permute-done | bytes 147488 | tf_op jit(solution)/shard_map/ppermute | solution.py:45
  27.1 2.8 %collective-permute-done.4.refs_4_ = bf16[288,256]{1,0:T(8,128)(2,1)S(1)} collective-permute-done((bf16[288,256]{1,0:T(8,128)(2,1)S(1)}, bf16[288,256]{1,0:T(8,128)(2,1)S(1)}, u32[]{:S(2)}, u32[]{:S(2)}) %collective-permute-start.4) | collective-permute-done | bytes 147488 | tf_op jit(solution)/shard_map/ppermute | solution.py:45
  29.9 0.1 plane.1.refs_0_
  29.9 1.6 %collective-permute-start.6 = (bf16[1040,256]{1,0:T(8,128)(2,1)S(1)}, bf16[1040,256]{1,0:T(8,128)(2,1)S(1)}, u32[]{:S(2)}, u32[]{:S(2)}) collective-permute-start(bf16[1040,256]{1,0:T(8,128)(2,1)S(1)} %plane.1.refs_0_), channel_id=1, source_target_pairs={{0,16},{1,17},{2,18},{3,19},{4,20},{5,21},{6,22},{7,23},{8,24},{9,... | collective-permute-start | bytes 1597448 | tf_op jit(solution)/shard_map/ppermute | solution.py:45
  31.5 1.7 %collective-permute-start.7 = (bf16[1040,256]{1,0:T(8,128)(2,1)S(1)}, bf16[1040,256]{1,0:T(8,128)(2,1)S(1)}, u32[]{:S(2)}, u32[]{:S(2)}) collective-permute-start(bf16[1040,256]{1,0:T(8,128)(2,1)S(1)} %plane.1.refs_0_), channel_id=1, source_target_pairs={{0,48},{1,49},{2,50},{3,51},{4,52},{5,53},{6,54},{7,55},{8,56},{9,... | collective-permute-start | bytes 1597448 | tf_op jit(solution)/shard_map/ppermute | solution.py:45
  33.2 0.4 collective-permute-start.10
  33.7 1.8 %collective-permute-start.8 = (bf16[1040,256]{1,0:T(8,128)(2,1)S(1)}, bf16[1040,256]{1,0:T(8,128)(2,1)S(1)}, u32[]{:S(2)}, u32[]{:S(2)}) collective-permute-start(bf16[1040,256]{1,0:T(8,128)(2,1)S(1)} %plane.1.refs_0_), channel_id=1, source_target_pairs={{0,32},{1,33},{2,34},{3,35},{4,36},{5,37},{6,38},{7,39},{8,40},{9,... | collective-permute-start | bytes 1597448 | tf_op jit(solution)/shard_map/ppermute | solution.py:45
  35.5 0.0 collective-permute-done.9.rows
  35.5 0.2 other_rows.2
  35.7 15.4 %row_statistics.4.refs_2_ = f32[16,3072]{1,0:T(8,128)S(1)} custom-call(s32[5]{0:T(128)S(1)} %get-tuple-element.52.meta, bf16[1040,256]{1,0:T(8,128)(2,1)S(1)} %plane.1.refs_0_, bf16[128,3072]{1,0:T(8,128)(2,1)S(1)} %get-tuple-element.73.refs_1_.qt), custom_call_target="tpu_custom_call" | custom-call | flops 2000000000 | bytes 100000 | tf_op jit(solution)/shard_map/row_statistics/pallas_call | solution.py:368
  51.1 4.3 %row_statistics.5.refs_2_ = f32[16,3072]{1,0:T(8,128)S(1)} custom-call(s32[5]{0:T(128)S(1)} %get-tuple-element.52.meta, bf16[1040,256]{1,0:T(8,128)(2,1)S(1)} %collective-permute-done.6.refs_1_.refs_0_, bf16[128,3072]{1,0:T(8,128)(2,1)S(1)} %get-tuple-element.73.refs_1_.qt, f32[16,3072]{1,0:T(8,128)S(1)} %row_statistics.4.refs_2_), custom_call_target="tpu_custom_call" | custom-call | flops 2000000000 | bytes 100000 | tf_op jit(solution)/shard_map/row_statistics/pallas_call | solution.py:368
  55.4 0.0 collective-permute-done.7.refs_2_.refs_0_
  55.4 4.1 %row_statistics.6.refs_2_ = f32[16,3072]{1,0:T(8,128)S(1)} custom-call(s32[5]{0:T(128)S(1)} %get-tuple-element.52.meta, bf16[1040,256]{1,0:T(8,128)(2,1)S(1)} %collective-permute-done.7.refs_2_.refs_0_, bf16[128,3072]{1,0:T(8,128)(2,1)S(1)} %get-tuple-element.73.refs_1_.qt, f32[16,3072]{1,0:T(8,128)S(1)} %row_statistics.5.refs_2_), custom_call_target="tpu_custom_call" | custom-call | flops 2000000000 | bytes 100000 | tf_op jit(solution)/shard_map/row_statistics/pallas_call | solution.py:368
  59.6 4.2 %row_statistics.7.mine_ref = f32[8,3072]{1,0:T(8,128)S(1)} custom-call(s32[5]{0:T(128)S(1)} %get-tuple-element.52.meta, bf16[1040,256]{1,0:T(8,128)(2,1)S(1)} %collective-permute-done.8.refs_3_.refs_0_, bf16[128,3072]{1,0:T(8,128)(2,1)S(1)} %get-tuple-element.73.refs_1_.qt, f32[16,3072]{1,0:T(8,128)S(1)} %row_statistics.6.refs_2_, ...), custom_call_target="tpu_custom_call" | custom-call | flops 2000000000 | bytes 100000 | tf_op jit(solution)/shard_map/row_statistics/pallas_call | solution.py:368
  63.7 1.7 %collective-permute-start.11 = (f32[8,3072]{1,0:T(8,128)S(1)}, f32[8,3072]{1,0:T(8,128)S(1)}, u32[]{:S(2)}, u32[]{:S(2)}) collective-permute-start(f32[8,3072]{1,0:T(8,128)S(1)} %row_statistics.7.mine_ref), channel_id=1, source_target_pairs={{0,1},{1,0},{2,3},{3,2},{4,5},{5,4},{6,7},{7,6},{8,9},{9,8},{10,11... | collective-permute-start | bytes 294920 | tf_op jit(solution)/shard_map/ppermute | solution.py:45
  65.4 0.2 other_rows.3
  65.6 0.8 sort.1
  66.4 2.0 %collective-permute-done.11.other_ref = f32[8,3072]{1,0:T(8,128)S(1)} collective-permute-done((f32[8,3072]{1,0:T(8,128)S(1)}, f32[8,3072]{1,0:T(8,128)S(1)}, u32[]{:S(2)}, u32[]{:S(2)}) %collective-permute-start.11) | collective-permute-done | bytes 98336 | tf_op jit(solution)/shard_map/ppermute | solution.py:45
  68.4 8.0 %gradients.3 = (f32[4096,256]{1,0:T(8,128)S(1)}, f32[128,3072]{1,0:T(8,128)S(1)}, bf16[1024,256]{1,0:T(8,128)(2,1)S(1)}) custom-call(s32[5]{0:T(128)S(1)} %get-tuple-element.52.meta, bf16[4096,256]{1,0:T(8,128)(2,1)S(1)} %get-tuple-element.66.pairs, bf16[3072,128]{1,0:T(8,128)(2,1)S(1)} %get-tuple-element.69.qs, ...), custom_call_target="tpu_custom_call", output_to_operand_aliasing={{0}: (8, {}), {1}: (9, {})} | custom-call | flops 8000000000 | bytes 100000 | tf_op jit(solution)/shard_map/gradients/pallas_call | solution.py:368
  76.5 1.4 collective-permute-start.12
  77.8 8.1 %gradients.4 = (f32[4096,256]{1,0:T(8,128)S(1)}, f32[128,3072]{1,0:T(8,128)S(1)}, bf16[1024,256]{1,0:T(8,128)(2,1)S(1)}, bf16[1024,256]{1,0:T(8,128)(2,1)S(1)}) custom-call(s32[5]{0:T(128)S(1)} %get-tuple-element.52.meta, bf16[4096,256]{1,0:T(8,128)(2,1)S(1)} %get-tuple-element.66.pairs, ...), custom_call_target="tpu_custom_call", output_to_operand_aliasing={{0}: (8, {}), {1}: (9, {})} | custom-call | flops 8000000000 | bytes 100000 | tf_op jit(solution)/shard_map/gradients/pallas_call | solution.py:368
  85.9 2.6 %collective-permute-start.13 = (bf16[1024,256]{1,0:T(8,128)(2,1)S(1)}, bf16[1024,256]{1,0:T(8,128)(2,1)S(1)}, u32[]{:S(2)}, u32[]{:S(2)}) collective-permute-start(bf16[1024,256]{1,0:T(8,128)(2,1)S(1)} %get-tuple-element.87), channel_id=1, source_target_pairs={{0,16},{1,17},{2,18},{3,19},{4,20},{5,21},{6,22},{7,23},{8,24},{9,... | collective-permute-start | bytes 1572872 | tf_op jit(solution)/shard_map/ppermute | solution.py:45
  88.6 2.9 %collective-permute-start.14 = (bf16[1024,256]{1,0:T(8,128)(2,1)S(1)}, bf16[1024,256]{1,0:T(8,128)(2,1)S(1)}, u32[]{:S(2)}, u32[]{:S(2)}) collective-permute-start(bf16[1024,256]{1,0:T(8,128)(2,1)S(1)} %get-tuple-element.88), channel_id=1, source_target_pairs={{0,48},{1,49},{2,50},{3,51},{4,52},{5,53},{6,54},{7,55},{8,56},{9,... | collective-permute-start | bytes 1572872 | tf_op jit(solution)/shard_map/ppermute | solution.py:45
  91.5 0.0 collective-permute-done.12
  91.5 8.0 %gradients.5 = (f32[4096,256]{1,0:T(8,128)S(1)}, f32[128,3072]{1,0:T(8,128)S(1)}, f32[1024,256]{1,0:T(8,128)S(1)}) custom-call(s32[5]{0:T(128)S(1)} %get-tuple-element.52.meta, bf16[4096,256]{1,0:T(8,128)(2,1)S(1)} %get-tuple-element.66.pairs, bf16[3072,128]{1,0:T(8,128)(2,1)S(1)} %get-tuple-element.69.qs, ...), custom_call_target="tpu_custom_call", output_to_operand_aliasing={{0}: (8, {}), {1}: (9, {})} | custom-call | flops 8000000000 | bytes 100000 | tf_op jit(solution)/shard_map/gradients/pallas_call | solution.py:368
  99.6 0.5 d_queries.1
  100.0 1.0 collective-permute-done.14
  101.1 0.3 convert_add_fusion
  101.3 0.1 convert.4
  101.4 15.6 %collective-permute-start.15 = (bf16[256,256]{1,0:T(8,128)(2,1)S(1)}, bf16[256,256]{1,0:T(8,128)(2,1)S(1)}, u32[]{:S(2)}, u32[]{:S(2)}) collective-permute-start(bf16[256,256]{1,0:T(8,128)(2,1)S(1)} %get-tuple-element.100), channel_id=1, source_target_pairs={{0,2},{1,3},{2,4},{3,5},{4,6},{5,7},{6,8},{7,9},{8,10},{9,11},{10,... | collective-permute-start | bytes 393224 | tf_op jit(solution)/shard_map/ppermute | solution.py:45
  117.0 9.4 %collective-permute-start.16 = (bf16[256,256]{1,0:T(8,128)(2,1)S(1)}, bf16[256,256]{1,0:T(8,128)(2,1)S(1)}, u32[]{:S(2)}, u32[]{:S(2)}) collective-permute-start(bf16[256,256]{1,0:T(8,128)(2,1)S(1)} %get-tuple-element.101), channel_id=1, source_target_pairs={{0,14},{1,15},{2,0},{3,1},{4,2},{5,3},{6,4},{7,5},{8,6},{9,7},{10,... | collective-permute-start | bytes 393224 | tf_op jit(solution)/shard_map/ppermute | solution.py:45
  126.4 2.0 %collective-permute-start.20 = (bf16[128,1536]{1,0:T(8,128)(2,1)S(1)}, bf16[128,1536]{1,0:T(8,128)(2,1)S(1)}, u32[]{:S(2)}, u32[]{:S(2)}) collective-permute-start(bf16[128,1536]{1,0:T(8,128)(2,1)S(1)} %get-tuple-element.94), channel_id=1, source_target_pairs={{0,1},{1,0},{2,3},{3,2},{4,5},{5,4},{6,7},{7,6},{8,9},{9,8},{10,11... | collective-permute-start | bytes 1179656 | tf_op jit(solution)/shard_map/ppermute | solution.py:45
  128.4 2.5 %collective-permute-done.15 = bf16[256,256]{1,0:T(8,128)(2,1)S(1)} collective-permute-done((bf16[256,256]{1,0:T(8,128)(2,1)S(1)}, bf16[256,256]{1,0:T(8,128)(2,1)S(1)}, u32[]{:S(2)}, u32[]{:S(2)}) %collective-permute-start.15) | collective-permute-done | bytes 131104 | tf_op jit(solution)/shard_map/ppermute | solution.py:45
  131.0 0.1 fusion.2
  131.1 4.6 %collective-permute-start.17 = (bf16[128,256]{1,0:T(8,128)(2,1)S(1)}, bf16[128,256]{1,0:T(8,128)(2,1)S(1)}, u32[]{:S(2)}, u32[]{:S(2)}) collective-permute-start(bf16[128,256]{1,0:T(8,128)(2,1)S(1)} %get-tuple-element.97), channel_id=1, source_target_pairs={{0,8},{1,9},{2,10},{3,11},{4,12},{5,13},{6,14},{7,15},{8,0},{9,1},... | collective-permute-start | bytes 196616 | tf_op jit(solution)/shard_map/ppermute | solution.py:45
  135.6 0.0 collective-permute-start.18
  135.6 3.2 %collective-permute-start.19 = (bf16[128,256]{1,0:T(8,128)(2,1)S(1)}, bf16[128,256]{1,0:T(8,128)(2,1)S(1)}, u32[]{:S(2)}, u32[]{:S(2)}) collective-permute-start(bf16[128,256]{1,0:T(8,128)(2,1)S(1)} %get-tuple-element.99), channel_id=1, source_target_pairs={{0,14},{1,15},{2,0},{3,1},{4,2},{5,3},{6,4},{7,5},{8,6},{9,7},{10,... | collective-permute-start | bytes 196616 | tf_op jit(solution)/shard_map/ppermute | solution.py:45
  138.9 0.6 collective-permute-done.17
  139.4 1.7 %collective-permute-done.18 = bf16[128,256]{1,0:T(8,128)(2,1)S(1)} collective-permute-done((bf16[128,256]{1,0:T(8,128)(2,1)S(1)}, bf16[128,256]{1,0:T(8,128)(2,1)S(1)}, u32[]{:S(2)}, u32[]{:S(2)}) %collective-permute-start.18) | collective-permute-done | bytes 65568 | tf_op jit(solution)/shard_map/ppermute | solution.py:45
  141.1 0.0 collective-permute-done.19
  141.1 0.0 collective-permute-done.20
  141.2 1.5 %collective-permute-start.21 = (f32[64,256]{1,0:T(8,128)S(1)}, f32[64,256]{1,0:T(8,128)S(1)}, u32[]{:S(2)}, u32[]{:S(2)}) collective-permute-start(f32[64,256]{1,0:T(8,128)S(1)} %get-tuple-element.105), channel_id=1, source_target_pairs={{0,1},{1,0},{2,3},{3,2},{4,5},{5,4},{6,7},{7,6},{8,9},{9,8},{10,11... | collective-permute-start | bytes 196616 | tf_op jit(solution)/shard_map/ppermute | solution.py:45
  142.6 0.8 add_convert_fusion
  143.4 2.1 %collective-permute-done.21 = f32[64,256]{1,0:T(8,128)S(1)} collective-permute-done((f32[64,256]{1,0:T(8,128)S(1)}, f32[64,256]{1,0:T(8,128)S(1)}, u32[]{:S(2)}, u32[]{:S(2)}) %collective-permute-start.21) | collective-permute-done | bytes 65568 | tf_op jit(solution)/shard_map/ppermute | solution.py:45
  145.5 0.7 fusion.4
  (20 shorter events, 0.2 us)
Async XLA Ops:
  0.7 0.8 copy-start
  1.5 0.8 copy-start.1
  2.3 0.7 copy-start.2
  3.6 4.3 %collective-permute-start = (bf16[80,256]{1,0:T(8,128)(2,1)S(1)}, bf16[80,256]{1,0:T(8,128)(2,1)S(1)}, u32[]{:S(2)}, u32[]{:S(2)}) collective-permute-start(bf16[80,256]{1,0:T(8,128)(2,1)S(1)} %get-tuple-element.51), channel_id=1, source_target_pairs={{0,1},{1,0},{2,3},{3,2},{4,5},{5,4},{6,7},{7,6},{8,9},{9,8},{10,11... | collective-permute-start | bytes 122888 | tf_op jit(solution)/shard_map/ppermute | solution.py:45
  9.0 12.7 %collective-permute-start.3 = (bf16[144,256]{1,0:T(8,128)(2,1)S(1)}, bf16[144,256]{1,0:T(8,128)(2,1)S(1)}, u32[]{:S(2)}, u32[]{:S(2)}) collective-permute-start(bf16[144,256]{1,0:T(8,128)(2,1)S(1)} %get-tuple-element.54.refs_0_), channel_id=1, source_target_pairs={{0,8},{1,9},{2,10},{3,11},{4,12},{5,13},{6,14},{7,15},{8,0},{9,1},... | collective-permute-start | bytes 221192 | tf_op jit(solution)/shard_map/ppermute | solution.py:45
  16.1 5.6 %collective-permute-start.2 = (bf16[144,256]{1,0:T(8,128)(2,1)S(1)}, bf16[144,256]{1,0:T(8,128)(2,1)S(1)}, u32[]{:S(2)}, u32[]{:S(2)}) collective-permute-start(bf16[144,256]{1,0:T(8,128)(2,1)S(1)} %get-tuple-element.54.refs_0_), channel_id=1, source_target_pairs={{0,14},{1,15},{2,0},{3,1},{4,2},{5,3},{6,4},{7,5},{8,6},{9,7},{10,... | collective-permute-start | bytes 221192 | tf_op jit(solution)/shard_map/ppermute | solution.py:45
  16.3 5.6 %collective-permute-start.1 = (bf16[144,256]{1,0:T(8,128)(2,1)S(1)}, bf16[144,256]{1,0:T(8,128)(2,1)S(1)}, u32[]{:S(2)}, u32[]{:S(2)}) collective-permute-start(bf16[144,256]{1,0:T(8,128)(2,1)S(1)} %get-tuple-element.54.refs_0_), channel_id=1, source_target_pairs={{0,2},{1,3},{2,4},{3,5},{4,6},{5,7},{6,8},{7,9},{8,10},{9,11},{10,... | collective-permute-start | bytes 221192 | tf_op jit(solution)/shard_map/ppermute | solution.py:45
  18.2 1.0 copy-start.3
  19.2 1.0 copy-start.4
  20.2 3.8 %copy-start.5 = (bf16[128,1536]{1,0:T(8,128)(2,1)S(1)}, bf16[128,1536]{1,0:T(8,128)(2,1)}, u32[]{:S(2)}) copy-start(bf16[128,1536]{1,0:T(8,128)(2,1)} %q_own) | copy-start | bytes 1179652
  21.8 5.2 %collective-permute-start.5 = (bf16[288,256]{1,0:T(8,128)(2,1)S(1)}, bf16[288,256]{1,0:T(8,128)(2,1)S(1)}, u32[]{:S(2)}, u32[]{:S(2)}) collective-permute-start(bf16[288,256]{1,0:T(8,128)(2,1)S(1)} %get-tuple-element.107), channel_id=1, source_target_pairs={{0,14},{1,15},{2,0},{3,1},{4,2},{5,3},{6,4},{7,5},{8,6},{9,7},{10,... | collective-permute-start | bytes 442376 | tf_op jit(solution)/shard_map/ppermute | solution.py:45
  23.5 6.4 %collective-permute-start.4 = (bf16[288,256]{1,0:T(8,128)(2,1)S(1)}, bf16[288,256]{1,0:T(8,128)(2,1)S(1)}, u32[]{:S(2)}, u32[]{:S(2)}) collective-permute-start(bf16[288,256]{1,0:T(8,128)(2,1)S(1)} %get-tuple-element.108), channel_id=1, source_target_pairs={{0,2},{1,3},{2,4},{3,5},{4,6},{5,7},{6,8},{7,9},{8,10},{9,11},{10,... | collective-permute-start | bytes 442376 | tf_op jit(solution)/shard_map/ppermute | solution.py:45
  23.9 11.5 %collective-permute-start.9 = (bf16[128,1536]{1,0:T(8,128)(2,1)S(1)}, bf16[128,1536]{1,0:T(8,128)(2,1)S(1)}, u32[]{:S(2)}, u32[]{:S(2)}) collective-permute-start(bf16[128,1536]{1,0:T(8,128)(2,1)S(1)} %copy-done.5), channel_id=1, source_target_pairs={{0,1},{1,0},{2,3},{3,2},{4,5},{5,4},{6,7},{7,6},{8,9},{9,8},{10,11... | collective-permute-start | bytes 1179656 | tf_op jit(solution)/shard_map/ppermute | solution.py:45
  29.9 21.1 %collective-permute-start.6 = (bf16[1040,256]{1,0:T(8,128)(2,1)S(1)}, bf16[1040,256]{1,0:T(8,128)(2,1)S(1)}, u32[]{:S(2)}, u32[]{:S(2)}) collective-permute-start(bf16[1040,256]{1,0:T(8,128)(2,1)S(1)} %plane.1.refs_0_), channel_id=1, source_target_pairs={{0,16},{1,17},{2,18},{3,19},{4,20},{5,21},{6,22},{7,23},{8,24},{9,... | collective-permute-start | bytes 1597448 | tf_op jit(solution)/shard_map/ppermute | solution.py:45
  31.5 23.9 %collective-permute-start.7 = (bf16[1040,256]{1,0:T(8,128)(2,1)S(1)}, bf16[1040,256]{1,0:T(8,128)(2,1)S(1)}, u32[]{:S(2)}, u32[]{:S(2)}) collective-permute-start(bf16[1040,256]{1,0:T(8,128)(2,1)S(1)} %plane.1.refs_0_), channel_id=1, source_target_pairs={{0,48},{1,49},{2,50},{3,51},{4,52},{5,53},{6,54},{7,55},{8,56},{9,... | collective-permute-start | bytes 1597448 | tf_op jit(solution)/shard_map/ppermute | solution.py:45
  33.2 32.2 %collective-permute-start.10 = (bf16[128,1536]{1,0:T(8,128)(2,1)}, bf16[128,1536]{1,0:T(8,128)(2,1)S(1)}, u32[]{:S(2)}, u32[]{:S(2)}) collective-permute-start(bf16[128,1536]{1,0:T(8,128)(2,1)} %g_own), channel_id=1, source_target_pairs={{0,1},{1,0},{2,3},{3,2},{4,5},{5,4},{6,7},{7,6},{8,9},{9,8},{10,11... | collective-permute-start | bytes 1179656 | tf_op jit(solution)/shard_map/ppermute | solution.py:45
  33.7 25.9 %collective-permute-start.8 = (bf16[1040,256]{1,0:T(8,128)(2,1)S(1)}, bf16[1040,256]{1,0:T(8,128)(2,1)S(1)}, u32[]{:S(2)}, u32[]{:S(2)}) collective-permute-start(bf16[1040,256]{1,0:T(8,128)(2,1)S(1)} %plane.1.refs_0_), channel_id=1, source_target_pairs={{0,32},{1,33},{2,34},{3,35},{4,36},{5,37},{6,38},{7,39},{8,40},{9,... | collective-permute-start | bytes 1597448 | tf_op jit(solution)/shard_map/ppermute | solution.py:45
  63.7 4.7 %collective-permute-start.11 = (f32[8,3072]{1,0:T(8,128)S(1)}, f32[8,3072]{1,0:T(8,128)S(1)}, u32[]{:S(2)}, u32[]{:S(2)}) collective-permute-start(f32[8,3072]{1,0:T(8,128)S(1)} %row_statistics.7.mine_ref), channel_id=1, source_target_pairs={{0,1},{1,0},{2,3},{3,2},{4,5},{5,4},{6,7},{7,6},{8,9},{9,8},{10,11... | collective-permute-start | bytes 294920 | tf_op jit(solution)/shard_map/ppermute | solution.py:45
  76.5 15.1 %collective-permute-start.12 = (bf16[1024,256]{1,0:T(8,128)(2,1)S(1)}, bf16[1024,256]{1,0:T(8,128)(2,1)S(1)}, u32[]{:S(2)}, u32[]{:S(2)}) collective-permute-start(bf16[1024,256]{1,0:T(8,128)(2,1)S(1)} %get-tuple-element.78), channel_id=1, source_target_pairs={{0,32},{1,33},{2,34},{3,35},{4,36},{5,37},{6,38},{7,39},{8,40},{9,... | collective-permute-start | bytes 1572872 | tf_op jit(solution)/shard_map/ppermute | solution.py:45
  85.9 14.1 %collective-permute-start.13 = (bf16[1024,256]{1,0:T(8,128)(2,1)S(1)}, bf16[1024,256]{1,0:T(8,128)(2,1)S(1)}, u32[]{:S(2)}, u32[]{:S(2)}) collective-permute-start(bf16[1024,256]{1,0:T(8,128)(2,1)S(1)} %get-tuple-element.87), channel_id=1, source_target_pairs={{0,16},{1,17},{2,18},{3,19},{4,20},{5,21},{6,22},{7,23},{8,24},{9,... | collective-permute-start | bytes 1572872 | tf_op jit(solution)/shard_map/ppermute | solution.py:45
  88.6 12.5 %collective-permute-start.14 = (bf16[1024,256]{1,0:T(8,128)(2,1)S(1)}, bf16[1024,256]{1,0:T(8,128)(2,1)S(1)}, u32[]{:S(2)}, u32[]{:S(2)}) collective-permute-start(bf16[1024,256]{1,0:T(8,128)(2,1)S(1)} %get-tuple-element.88), channel_id=1, source_target_pairs={{0,48},{1,49},{2,50},{3,51},{4,52},{5,53},{6,54},{7,55},{8,56},{9,... | collective-permute-start | bytes 1572872 | tf_op jit(solution)/shard_map/ppermute | solution.py:45
  101.4 29.5 %collective-permute-start.15 = (bf16[256,256]{1,0:T(8,128)(2,1)S(1)}, bf16[256,256]{1,0:T(8,128)(2,1)S(1)}, u32[]{:S(2)}, u32[]{:S(2)}) collective-permute-start(bf16[256,256]{1,0:T(8,128)(2,1)S(1)} %get-tuple-element.100), channel_id=1, source_target_pairs={{0,2},{1,3},{2,4},{3,5},{4,6},{5,7},{6,8},{7,9},{8,10},{9,11},{10,... | collective-permute-start | bytes 393224 | tf_op jit(solution)/shard_map/ppermute | solution.py:45
  117.0 13.9 %collective-permute-start.16 = (bf16[256,256]{1,0:T(8,128)(2,1)S(1)}, bf16[256,256]{1,0:T(8,128)(2,1)S(1)}, u32[]{:S(2)}, u32[]{:S(2)}) collective-permute-start(bf16[256,256]{1,0:T(8,128)(2,1)S(1)} %get-tuple-element.101), channel_id=1, source_target_pairs={{0,14},{1,15},{2,0},{3,1},{4,2},{5,3},{6,4},{7,5},{8,6},{9,7},{10,... | collective-permute-start | bytes 393224 | tf_op jit(solution)/shard_map/ppermute | solution.py:45
  126.4 14.7 %collective-permute-start.20 = (bf16[128,1536]{1,0:T(8,128)(2,1)S(1)}, bf16[128,1536]{1,0:T(8,128)(2,1)S(1)}, u32[]{:S(2)}, u32[]{:S(2)}) collective-permute-start(bf16[128,1536]{1,0:T(8,128)(2,1)S(1)} %get-tuple-element.94), channel_id=1, source_target_pairs={{0,1},{1,0},{2,3},{3,2},{4,5},{5,4},{6,7},{7,6},{8,9},{9,8},{10,11... | collective-permute-start | bytes 1179656 | tf_op jit(solution)/shard_map/ppermute | solution.py:45
  131.1 8.4 %collective-permute-start.17 = (bf16[128,256]{1,0:T(8,128)(2,1)S(1)}, bf16[128,256]{1,0:T(8,128)(2,1)S(1)}, u32[]{:S(2)}, u32[]{:S(2)}) collective-permute-start(bf16[128,256]{1,0:T(8,128)(2,1)S(1)} %get-tuple-element.97), channel_id=1, source_target_pairs={{0,8},{1,9},{2,10},{3,11},{4,12},{5,13},{6,14},{7,15},{8,0},{9,1},... | collective-permute-start | bytes 196616 | tf_op jit(solution)/shard_map/ppermute | solution.py:45
  135.6 5.5 %collective-permute-start.18 = (bf16[128,256]{1,0:T(8,128)(2,1)S(1)}, bf16[128,256]{1,0:T(8,128)(2,1)S(1)}, u32[]{:S(2)}, u32[]{:S(2)}) collective-permute-start(bf16[128,256]{1,0:T(8,128)(2,1)S(1)} %get-tuple-element.98), channel_id=1, source_target_pairs={{0,2},{1,3},{2,4},{3,5},{4,6},{5,7},{6,8},{7,9},{8,10},{9,11},{10,... | collective-permute-start | bytes 196616 | tf_op jit(solution)/shard_map/ppermute | solution.py:45
  135.6 5.5 %collective-permute-start.19 = (bf16[128,256]{1,0:T(8,128)(2,1)S(1)}, bf16[128,256]{1,0:T(8,128)(2,1)S(1)}, u32[]{:S(2)}, u32[]{:S(2)}) collective-permute-start(bf16[128,256]{1,0:T(8,128)(2,1)S(1)} %get-tuple-element.99), channel_id=1, source_target_pairs={{0,14},{1,15},{2,0},{3,1},{4,2},{5,3},{6,4},{7,5},{8,6},{9,7},{10,... | collective-permute-start | bytes 196616 | tf_op jit(solution)/shard_map/ppermute | solution.py:45
  141.2 4.4 %collective-permute-start.21 = (f32[64,256]{1,0:T(8,128)S(1)}, f32[64,256]{1,0:T(8,128)S(1)}, u32[]{:S(2)}, u32[]{:S(2)}) collective-permute-start(f32[64,256]{1,0:T(8,128)S(1)} %get-tuple-element.105), channel_id=1, source_target_pairs={{0,1},{1,0},{2,3},{3,2},{4,5},{5,4},{6,7},{7,6},{8,9},{9,8},{10,11... | collective-permute-start | bytes 196616 | tf_op jit(solution)/shard_map/ppermute | solution.py:45
where the time goes:
time: 149 us; the launch traced here: 146 us
  starting transfers between devices  64.4 us (43%)
  Pallas kernels  57.2 us (38%)
  waiting for transfers between devices  17.4 us (12%)
  local copies, waits for them, and re-layouts  4.19 us (3%)
  other arithmetic  2.04 us (1%)
    ppermute x22, starting transfers between devices, shift(): return lax.ppermute(block, 'ctx', pairs)  64.4 us
    pallas_call x15, Pallas kernels, run(): pl.pallas_call(kernel, out_shape=[jax.ShapeDtypeStruct(s, d) for s, d in...  57.2 us
    ppermute x22, waiting for transfers between devices, shift(): return lax.ppermute(block, 'ctx', pairs)  17.4 us
    unnamed x12, local copies, waits for them, and re-layouts  4.17 us
  transfers between devices with their start and end apart: 22, of which 10 were waited for; matrix products, arithmetic and copies ran while one was open for 1% of the time, Pallas kernels for 32%

commit v1 on v0

--- a/solution.py
+++ b/solution.py
@@ -470,9 +470,8 @@
     near, far, back = (shift(plane, dx=d) for d in range(1, NX))
     gathered = [plane, near, back, far]
     stats = None
-    for i, part in enumerate(gathered):
-        last = i == len(gathered) - 1
-        stats = statistics(meta, [part], qt, stats, delta if last else None)
+    for parts in ([plane], [near], [back, far]):
+        stats = statistics(meta, parts, qt, stats, delta if len(parts) == 2 else None)
     other_stats = shift(stats, dy=1)
     pairs, *state = run(
         functools.partial(sort_kernel, len(gathered)), [], gathered,

time: 149 us -> 152 us (1.020); the launches traced: 146 us -> 151 us
  waiting for transfers between devices: 17.4 us -> 27.9 us
  starting transfers between devices: 64.4 us -> 58.4 us
    ppermute x22, waiting for transfers between devices: 17.4 us -> 27.9 us  [shift(): return lax.ppermute(block, 'ctx', pairs)]
    ppermute x22, starting transfers between devices: 64.4 us -> 58.4 us  [shift(): return lax.ppermute(block, 'ctx', pairs)]
    pallas_call x15 -> x14, Pallas kernels: 57.2 us -> 57.8 us  [run(): pl.pallas_call(kernel, out_shape=[jax.ShapeDtypeStruct(s, d) for s, d in...]
  transfers between devices with their start and end apart: 22 -> 22, of which waited for: 10 -> 11; matrix products, arithmetic and copies ran while one was open for 1% -> 1% of each run, Pallas kernels for 32% -> 32%
where the time goes in v1:
time: 152 us; the launch traced here: 151 us
  starting transfers between devices  58.4 us (38%)
  Pallas kernels  57.8 us (38%)
  waiting for transfers between devices  27.9 us (18%)
  local copies, waits for them, and re-layouts  4.19 us (3%)
  other arithmetic  2.05 us (1%)
    ppermute x22, starting transfers between devices, shift(): return lax.ppermute(block, 'ctx', pairs)  58.4 us
    pallas_call x14, Pallas kernels, run(): pl.pallas_call(kernel, out_shape=[jax.ShapeDtypeStruct(s, d) for s, d in...  57.8 us
    ppermute x22, waiting for transfers between devices, shift(): return lax.ppermute(block, 'ctx', pairs)  27.9 us
    unnamed x12, local copies, waits for them, and re-layouts  4.17 us
  transfers between devices with their start and end apart: 22, of which 11 were waited for; matrix products, arithmetic and copies ran while one was open for 1% of the time, Pallas kernels for 32%

profile of v1, /device:TPU:8, one launch (start us, length us, event | category | flops | bytes accessed | tf_op | source)
XLA Modules:
  0.0 151.1 jit_solution(15632040314495112172)
XLA Ops:
  0.7 0.1 pad_add_fusion.where
  0.7 0.8 copy-done
  1.5 0.8 copy-done.1
  2.3 0.7 copy-done.2
  2.9 0.7 pack.1
  3.6 2.3 %collective-permute-start = (bf16[80,256]{1,0:T(8,128)(2,1)S(1)}, bf16[80,256]{1,0:T(8,128)(2,1)S(1)}, u32[]{:S(2)}, u32[]{:S(2)}) collective-permute-start(bf16[80,256]{1,0:T(8,128)(2,1)S(1)} %get-tuple-element.51), channel_id=1, source_target_pairs={{0,1},{1,0},{2,3},{3,2},{4,5},{5,4},{6,7},{7,6},{8,9},{9,8},{10,11... | collective-permute-start | bytes 122888 | tf_op jit(solution)/shard_map/ppermute | solution.py:45
  5.9 2.0 %collective-permute-done.given = bf16[80,256]{1,0:T(8,128)(2,1)S(1)} collective-permute-done((bf16[80,256]{1,0:T(8,128)(2,1)S(1)}, bf16[80,256]{1,0:T(8,128)(2,1)S(1)}, u32[]{:S(2)}, u32[]{:S(2)}) %collective-permute-start) | collective-permute-done | bytes 40992 | tf_op jit(solution)/shard_map/ppermute | solution.py:45
  7.8 1.2 join.1
  9.0 7.1 %collective-permute-start.3 = (bf16[144,256]{1,0:T(8,128)(2,1)S(1)}, bf16[144,256]{1,0:T(8,128)(2,1)S(1)}, u32[]{:S(2)}, u32[]{:S(2)}) collective-permute-start(bf16[144,256]{1,0:T(8,128)(2,1)S(1)} %get-tuple-element.54.refs_0_), channel_id=1, source_target_pairs={{0,8},{1,9},{2,10},{3,11},{4,12},{5,13},{6,14},{7,15},{8,0},{9,1},... | collective-permute-start | bytes 221192 | tf_op jit(solution)/shard_map/ppermute | solution.py:45
  16.1 0.1 collective-permute-start.2
  16.3 1.9 %collective-permute-start.1 = (bf16[144,256]{1,0:T(8,128)(2,1)S(1)}, bf16[144,256]{1,0:T(8,128)(2,1)S(1)}, u32[]{:S(2)}, u32[]{:S(2)}) collective-permute-start(bf16[144,256]{1,0:T(8,128)(2,1)S(1)} %get-tuple-element.54.refs_0_), channel_id=1, source_target_pairs={{0,2},{1,3},{2,4},{3,5},{4,6},{5,7},{6,8},{7,9},{8,10},{9,11},{10,... | collective-permute-start | bytes 221192 | tf_op jit(solution)/shard_map/ppermute | solution.py:45
  18.2 1.0 copy-done.3
  19.2 1.0 copy-done.4
  20.2 1.5 %own_rows.1 = (bf16[3072,128]{1,0:T(8,128)(2,1)S(1)}, bf16[3072,128]{1,0:T(8,128)(2,1)S(1)}, bf16[128,3072]{1,0:T(8,128)(2,1)S(1)}, bf16[128,3072]{1,0:T(8,128)(2,1)S(1)}, f32[8,1536]{1,0:T(8,128)S(1)}) custom-call(bf16[128,1536]{1,0:T(8,128)(2,1)S(1)} %copy-done.4, bf16[128,1536]{1,0:T(8,128)(2,1)} %g_own, bf16[128,1536]{1,0:T(8,128)(2,1)S(1)} %copy-done.3), custom_call_target="tpu_custom_call" | custom-call | flops 1000000000 | bytes 100000 | tf_op jit(solution)/shard_map/own_rows/pallas_call | solution.py:368
  21.7 0.0 collective-permute-done.3.refs_1_
  21.7 0.0 collective-permute-done.2.refs_3_
  21.7 0.1 collective-permute-done.1.refs_2_
  21.8 1.7 %collective-permute-start.5 = (bf16[288,256]{1,0:T(8,128)(2,1)S(1)}, bf16[288,256]{1,0:T(8,128)(2,1)S(1)}, u32[]{:S(2)}, u32[]{:S(2)}) collective-permute-start(bf16[288,256]{1,0:T(8,128)(2,1)S(1)} %get-tuple-element.107), channel_id=1, source_target_pairs={{0,14},{1,15},{2,0},{3,1},{4,2},{5,3},{6,4},{7,5},{8,6},{9,7},{10,... | collective-permute-start | bytes 442376 | tf_op jit(solution)/shard_map/ppermute | solution.py:45
  23.5 0.4 collective-permute-start.4
  23.9 0.4 collective-permute-start.9
  24.4 2.7 %collective-permute-done.5.refs_5_ = bf16[288,256]{1,0:T(8,128)(2,1)S(1)} collective-permute-done((bf16[288,256]{1,0:T(8,128)(2,1)S(1)}, bf16[288,256]{1,0:T(8,128)(2,1)S(1)}, u32[]{:S(2)}, u32[]{:S(2)}) %collective-permute-start.5) | collective-permute-done | bytes 147488 | tf_op jit(solution)/shard_map/ppermute | solution.py:45
  27.1 2.8 %collective-permute-done.4.refs_4_ = bf16[288,256]{1,0:T(8,128)(2,1)S(1)} collective-permute-done((bf16[288,256]{1,0:T(8,128)(2,1)S(1)}, bf16[288,256]{1,0:T(8,128)(2,1)S(1)}, u32[]{:S(2)}, u32[]{:S(2)}) %collective-permute-start.4) | collective-permute-done | bytes 147488 | tf_op jit(solution)/shard_map/ppermute | solution.py:45
  29.9 0.1 plane.1.refs_0_
  29.9 1.6 %collective-permute-start.6 = (bf16[1040,256]{1,0:T(8,128)(2,1)S(1)}, bf16[1040,256]{1,0:T(8,128)(2,1)S(1)}, u32[]{:S(2)}, u32[]{:S(2)}) collective-permute-start(bf16[1040,256]{1,0:T(8,128)(2,1)S(1)} %plane.1.refs_0_), channel_id=1, source_target_pairs={{0,16},{1,17},{2,18},{3,19},{4,20},{5,21},{6,22},{7,23},{8,24},{9,... | collective-permute-start | bytes 1597448 | tf_op jit(solution)/shard_map/ppermute | solution.py:45
  31.5 2.7 %collective-permute-start.8 = (bf16[1040,256]{1,0:T(8,128)(2,1)S(1)}, bf16[1040,256]{1,0:T(8,128)(2,1)S(1)}, u32[]{:S(2)}, u32[]{:S(2)}) collective-permute-start(bf16[1040,256]{1,0:T(8,128)(2,1)S(1)} %plane.1.refs_0_), channel_id=1, source_target_pairs={{0,32},{1,33},{2,34},{3,35},{4,36},{5,37},{6,38},{7,39},{8,40},{9,... | collective-permute-start | bytes 1597448 | tf_op jit(solution)/shard_map/ppermute | solution.py:45
  34.2 1.4 collective-permute-start.7
  35.6 0.4 collective-permute-start.10
  36.1 0.0 collective-permute-done.9.rows
  36.1 0.2 other_rows.2
  36.3 19.7 %row_statistics.3.refs_2_ = f32[16,3072]{1,0:T(8,128)S(1)} custom-call(s32[5]{0:T(128)S(1)} %get-tuple-element.52.meta, bf16[1040,256]{1,0:T(8,128)(2,1)S(1)} %plane.1.refs_0_, bf16[128,3072]{1,0:T(8,128)(2,1)S(1)} %get-tuple-element.73.refs_1_.refs_2_.qt), custom_call_target="tpu_custom_call" | custom-call | flops 2000000000 | bytes 100000 | tf_op jit(solution)/shard_map/row_statistics/pallas_call | solution.py:368
  56.0 0.0 collective-permute-done.6.refs_1_.refs_0_
  56.0 3.4 %row_statistics.4.refs_3_ = f32[16,3072]{1,0:T(8,128)S(1)} custom-call(s32[5]{0:T(128)S(1)} %get-tuple-element.52.meta, bf16[1040,256]{1,0:T(8,128)(2,1)S(1)} %collective-permute-done.6.refs_1_.refs_0_, bf16[128,3072]{1,0:T(8,128)(2,1)S(1)} %get-tuple-element.73.refs_1_.refs_2_.qt, f32[16,3072]{1,0:T(8,128)S(1)} %row_statistics.3.refs_2_), custom_call_target="tpu_custom_call" | custom-call | flops 2000000000 | bytes 100000 | tf_op jit(solution)/shard_map/row_statistics/pallas_call | solution.py:368
  59.5 6.5 %row_statistics.5.mine_ref = f32[8,3072]{1,0:T(8,128)S(1)} custom-call(s32[5]{0:T(128)S(1)} %get-tuple-element.52.meta, bf16[1040,256]{1,0:T(8,128)(2,1)S(1)} %collective-permute-done.7.refs_2_.refs_0_, bf16[1040,256]{1,0:T(8,128)(2,1)S(1)} %collective-permute-done.8.refs_3_.refs_1_, bf16[128,3072]{1,0:T(8,128)(2,1)S(1)} %get-tuple-element.73.refs_1_.refs_2_.qt, ...), custom_call_target="tpu_custom_call" | custom-call | flops 2000000000 | bytes 100000 | tf_op jit(solution)/shard_map/row_statistics/pallas_call | solution.py:368
  66.0 16.3 %collective-permute-start.11 = (f32[8,3072]{1,0:T(8,128)S(1)}, f32[8,3072]{1,0:T(8,128)S(1)}, u32[]{:S(2)}, u32[]{:S(2)}) collective-permute-start(f32[8,3072]{1,0:T(8,128)S(1)} %row_statistics.5.mine_ref), channel_id=1, source_target_pairs={{0,1},{1,0},{2,3},{3,2},{4,5},{5,4},{6,7},{7,6},{8,9},{9,8},{10,11... | collective-permute-start | bytes 294920 | tf_op jit(solution)/shard_map/ppermute | solution.py:45
  82.3 0.0 collective-permute-done.10.rows
  82.3 0.2 other_rows.3
  82.5 0.8 sort.1
  83.4 1.6 %collective-permute-done.11.other_ref = f32[8,3072]{1,0:T(8,128)S(1)} collective-permute-done((f32[8,3072]{1,0:T(8,128)S(1)}, f32[8,3072]{1,0:T(8,128)S(1)}, u32[]{:S(2)}, u32[]{:S(2)}) %collective-permute-start.11) | collective-permute-done | bytes 98336 | tf_op jit(solution)/shard_map/ppermute | solution.py:45
  84.9 8.1 %gradients.3 = (f32[4096,256]{1,0:T(8,128)S(1)}, f32[128,3072]{1,0:T(8,128)S(1)}, bf16[1024,256]{1,0:T(8,128)(2,1)S(1)}) custom-call(s32[5]{0:T(128)S(1)} %get-tuple-element.52.meta, bf16[4096,256]{1,0:T(8,128)(2,1)S(1)} %get-tuple-element.66.pairs, bf16[3072,128]{1,0:T(8,128)(2,1)S(1)} %get-tuple-element.69.qs, ...), custom_call_target="tpu_custom_call", output_to_operand_aliasing={{0}: (8, {}), {1}: (9, {})} | custom-call | flops 8000000000 | bytes 100000 | tf_op jit(solution)/shard_map/gradients/pallas_call | solution.py:368
  93.0 0.1 collective-permute-start.12
  93.1 8.1 %gradients.4 = (f32[4096,256]{1,0:T(8,128)S(1)}, f32[128,3072]{1,0:T(8,128)S(1)}, bf16[1024,256]{1,0:T(8,128)(2,1)S(1)}, bf16[1024,256]{1,0:T(8,128)(2,1)S(1)}) custom-call(s32[5]{0:T(128)S(1)} %get-tuple-element.52.meta, bf16[4096,256]{1,0:T(8,128)(2,1)S(1)} %get-tuple-element.66.pairs, ...), custom_call_target="tpu_custom_call", output_to_operand_aliasing={{0}: (8, {}), {1}: (9, {})} | custom-call | flops 8000000000 | bytes 100000 | tf_op jit(solution)/shard_map/gradients/pallas_call | solution.py:368
  101.2 0.9 collective-permute-start.13
  102.1 2.4 %collective-permute-start.14 = (bf16[1024,256]{1,0:T(8,128)(2,1)S(1)}, bf16[1024,256]{1,0:T(8,128)(2,1)S(1)}, u32[]{:S(2)}, u32[]{:S(2)}) collective-permute-start(bf16[1024,256]{1,0:T(8,128)(2,1)S(1)} %get-tuple-element.88), channel_id=1, source_target_pairs={{0,48},{1,49},{2,50},{3,51},{4,52},{5,53},{6,54},{7,55},{8,56},{9,... | collective-permute-start | bytes 1572872 | tf_op jit(solution)/shard_map/ppermute | solution.py:45
  104.5 4.6 %collective-permute-done.12 = bf16[1024,256]{1,0:T(8,128)(2,1)S(1)} collective-permute-done((bf16[1024,256]{1,0:T(8,128)(2,1)S(1)}, bf16[1024,256]{1,0:T(8,128)(2,1)S(1)}, u32[]{:S(2)}, u32[]{:S(2)}) %collective-permute-start.12) | collective-permute-done | bytes 524320 | tf_op jit(solution)/shard_map/ppermute | solution.py:45
  109.1 6.8 %gradients.5 = (f32[4096,256]{1,0:T(8,128)S(1)}, f32[128,3072]{1,0:T(8,128)S(1)}, f32[1024,256]{1,0:T(8,128)S(1)}) custom-call(s32[5]{0:T(128)S(1)} %get-tuple-element.52.meta, bf16[4096,256]{1,0:T(8,128)(2,1)S(1)} %get-tuple-element.66.pairs, bf16[3072,128]{1,0:T(8,128)(2,1)S(1)} %get-tuple-element.69.qs, ...), custom_call_target="tpu_custom_call", output_to_operand_aliasing={{0}: (8, {}), {1}: (9, {})} | custom-call | flops 8000000000 | bytes 100000 | tf_op jit(solution)/shard_map/gradients/pallas_call | solution.py:368
  116.0 0.5 d_queries.1
  116.5 0.3 convert_add_fusion
  116.8 0.1 convert.4
  116.9 9.2 %collective-permute-start.15 = (bf16[256,256]{1,0:T(8,128)(2,1)S(1)}, bf16[256,256]{1,0:T(8,128)(2,1)S(1)}, u32[]{:S(2)}, u32[]{:S(2)}) collective-permute-start(bf16[256,256]{1,0:T(8,128)(2,1)S(1)} %get-tuple-element.100), channel_id=1, source_target_pairs={{0,2},{1,3},{2,4},{3,5},{4,6},{5,7},{6,8},{7,9},{8,10},{9,11},{10,... | collective-permute-start | bytes 393224 | tf_op jit(solution)/shard_map/ppermute | solution.py:45
  126.0 0.7 collective-permute-start.16
  126.7 2.2 %collective-permute-start.20 = (bf16[128,1536]{1,0:T(8,128)(2,1)S(1)}, bf16[128,1536]{1,0:T(8,128)(2,1)S(1)}, u32[]{:S(2)}, u32[]{:S(2)}) collective-permute-start(bf16[128,1536]{1,0:T(8,128)(2,1)S(1)} %get-tuple-element.94), channel_id=1, source_target_pairs={{0,1},{1,0},{2,3},{3,2},{4,5},{5,4},{6,7},{7,6},{8,9},{9,8},{10,11... | collective-permute-start | bytes 1179656 | tf_op jit(solution)/shard_map/ppermute | solution.py:45
  129.0 1.9 %collective-permute-done.15 = bf16[256,256]{1,0:T(8,128)(2,1)S(1)} collective-permute-done((bf16[256,256]{1,0:T(8,128)(2,1)S(1)}, bf16[256,256]{1,0:T(8,128)(2,1)S(1)}, u32[]{:S(2)}, u32[]{:S(2)}) %collective-permute-start.15) | collective-permute-done | bytes 131104 | tf_op jit(solution)/shard_map/ppermute | solution.py:45
  130.8 5.4 %collective-permute-done.16 = bf16[256,256]{1,0:T(8,128)(2,1)S(1)} collective-permute-done((bf16[256,256]{1,0:T(8,128)(2,1)S(1)}, bf16[256,256]{1,0:T(8,128)(2,1)S(1)}, u32[]{:S(2)}, u32[]{:S(2)}) %collective-permute-start.16) | collective-permute-done | bytes 131104 | tf_op jit(solution)/shard_map/ppermute | solution.py:45
  136.2 0.1 fusion.2
  136.3 3.1 %collective-permute-start.17 = (bf16[128,256]{1,0:T(8,128)(2,1)S(1)}, bf16[128,256]{1,0:T(8,128)(2,1)S(1)}, u32[]{:S(2)}, u32[]{:S(2)}) collective-permute-start(bf16[128,256]{1,0:T(8,128)(2,1)S(1)} %get-tuple-element.97), channel_id=1, source_target_pairs={{0,8},{1,9},{2,10},{3,11},{4,12},{5,13},{6,14},{7,15},{8,0},{9,1},... | collective-permute-start | bytes 196616 | tf_op jit(solution)/shard_map/ppermute | solution.py:45
  139.3 3.2 %collective-permute-start.19 = (bf16[128,256]{1,0:T(8,128)(2,1)S(1)}, bf16[128,256]{1,0:T(8,128)(2,1)S(1)}, u32[]{:S(2)}, u32[]{:S(2)}) collective-permute-start(bf16[128,256]{1,0:T(8,128)(2,1)S(1)} %get-tuple-element.99), channel_id=1, source_target_pairs={{0,14},{1,15},{2,0},{3,1},{4,2},{5,3},{6,4},{7,5},{8,6},{9,7},{10,... | collective-permute-start | bytes 196616 | tf_op jit(solution)/shard_map/ppermute | solution.py:45
  142.6 2.4 %collective-permute-done.17 = bf16[128,256]{1,0:T(8,128)(2,1)S(1)} collective-permute-done((bf16[128,256]{1,0:T(8,128)(2,1)S(1)}, bf16[128,256]{1,0:T(8,128)(2,1)S(1)}, u32[]{:S(2)}, u32[]{:S(2)}) %collective-permute-start.17) | collective-permute-done | bytes 65568 | tf_op jit(solution)/shard_map/ppermute | solution.py:45
  145.0 1.1 collective-permute-done.18
  146.0 0.0 collective-permute-done.19
  146.1 0.0 collective-permute-done.20
  146.1 0.1 collective-permute-start.21
  146.2 0.8 add_convert_fusion
  147.0 3.4 %collective-permute-done.21 = f32[64,256]{1,0:T(8,128)S(1)} collective-permute-done((f32[64,256]{1,0:T(8,128)S(1)}, f32[64,256]{1,0:T(8,128)S(1)}, u32[]{:S(2)}, u32[]{:S(2)}) %collective-permute-start.21) | collective-permute-done | bytes 65568 | tf_op jit(solution)/shard_map/ppermute | solution.py:45
  150.5 0.7 fusion.4
  (19 shorter events, 0.2 us)
Async XLA Ops:
  0.7 0.8 copy-start
  1.5 0.8 copy-start.1
  2.3 0.7 copy-start.2
  3.6 4.3 %collective-permute-start = (bf16[80,256]{1,0:T(8,128)(2,1)S(1)}, bf16[80,256]{1,0:T(8,128)(2,1)S(1)}, u32[]{:S(2)}, u32[]{:S(2)}) collective-permute-start(bf16[80,256]{1,0:T(8,128)(2,1)S(1)} %get-tuple-element.51), channel_id=1, source_target_pairs={{0,1},{1,0},{2,3},{3,2},{4,5},{5,4},{6,7},{7,6},{8,9},{9,8},{10,11... | collective-permute-start | bytes 122888 | tf_op jit(solution)/shard_map/ppermute | solution.py:45
  9.0 12.7 %collective-permute-start.3 = (bf16[144,256]{1,0:T(8,128)(2,1)S(1)}, bf16[144,256]{1,0:T(8,128)(2,1)S(1)}, u32[]{:S(2)}, u32[]{:S(2)}) collective-permute-start(bf16[144,256]{1,0:T(8,128)(2,1)S(1)} %get-tuple-element.54.refs_0_), channel_id=1, source_target_pairs={{0,8},{1,9},{2,10},{3,11},{4,12},{5,13},{6,14},{7,15},{8,0},{9,1},... | collective-permute-start | bytes 221192 | tf_op jit(solution)/shard_map/ppermute | solution.py:45
  16.1 5.6 %collective-permute-start.2 = (bf16[144,256]{1,0:T(8,128)(2,1)S(1)}, bf16[144,256]{1,0:T(8,128)(2,1)S(1)}, u32[]{:S(2)}, u32[]{:S(2)}) collective-permute-start(bf16[144,256]{1,0:T(8,128)(2,1)S(1)} %get-tuple-element.54.refs_0_), channel_id=1, source_target_pairs={{0,14},{1,15},{2,0},{3,1},{4,2},{5,3},{6,4},{7,5},{8,6},{9,7},{10,... | collective-permute-start | bytes 221192 | tf_op jit(solution)/shard_map/ppermute | solution.py:45
  16.3 5.6 %collective-permute-start.1 = (bf16[144,256]{1,0:T(8,128)(2,1)S(1)}, bf16[144,256]{1,0:T(8,128)(2,1)S(1)}, u32[]{:S(2)}, u32[]{:S(2)}) collective-permute-start(bf16[144,256]{1,0:T(8,128)(2,1)S(1)} %get-tuple-element.54.refs_0_), channel_id=1, source_target_pairs={{0,2},{1,3},{2,4},{3,5},{4,6},{5,7},{6,8},{7,9},{8,10},{9,11},{10,... | collective-permute-start | bytes 221192 | tf_op jit(solution)/shard_map/ppermute | solution.py:45
  18.2 1.0 copy-start.3
  19.2 1.0 copy-start.4
  20.2 3.8 %copy-start.5 = (bf16[128,1536]{1,0:T(8,128)(2,1)S(1)}, bf16[128,1536]{1,0:T(8,128)(2,1)}, u32[]{:S(2)}) copy-start(bf16[128,1536]{1,0:T(8,128)(2,1)} %q_own) | copy-start | bytes 1179652
  21.8 5.2 %collective-permute-start.5 = (bf16[288,256]{1,0:T(8,128)(2,1)S(1)}, bf16[288,256]{1,0:T(8,128)(2,1)S(1)}, u32[]{:S(2)}, u32[]{:S(2)}) collective-permute-start(bf16[288,256]{1,0:T(8,128)(2,1)S(1)} %get-tuple-element.107), channel_id=1, source_target_pairs={{0,14},{1,15},{2,0},{3,1},{4,2},{5,3},{6,4},{7,5},{8,6},{9,7},{10,... | collective-permute-start | bytes 442376 | tf_op jit(solution)/shard_map/ppermute | solution.py:45
  23.5 6.4 %collective-permute-start.4 = (bf16[288,256]{1,0:T(8,128)(2,1)S(1)}, bf16[288,256]{1,0:T(8,128)(2,1)S(1)}, u32[]{:S(2)}, u32[]{:S(2)}) collective-permute-start(bf16[288,256]{1,0:T(8,128)(2,1)S(1)} %get-tuple-element.108), channel_id=1, source_target_pairs={{0,2},{1,3},{2,4},{3,5},{4,6},{5,7},{6,8},{7,9},{8,10},{9,11},{10,... | collective-permute-start | bytes 442376 | tf_op jit(solution)/shard_map/ppermute | solution.py:45
  23.9 12.1 %collective-permute-start.9 = (bf16[128,1536]{1,0:T(8,128)(2,1)S(1)}, bf16[128,1536]{1,0:T(8,128)(2,1)S(1)}, u32[]{:S(2)}, u32[]{:S(2)}) collective-permute-start(bf16[128,1536]{1,0:T(8,128)(2,1)S(1)} %copy-done.5), channel_id=1, source_target_pairs={{0,1},{1,0},{2,3},{3,2},{4,5},{5,4},{6,7},{7,6},{8,9},{9,8},{10,11... | collective-permute-start | bytes 1179656 | tf_op jit(solution)/shard_map/ppermute | solution.py:45
  29.9 26.1 %collective-permute-start.6 = (bf16[1040,256]{1,0:T(8,128)(2,1)S(1)}, bf16[1040,256]{1,0:T(8,128)(2,1)S(1)}, u32[]{:S(2)}, u32[]{:S(2)}) collective-permute-start(bf16[1040,256]{1,0:T(8,128)(2,1)S(1)} %plane.1.refs_0_), channel_id=1, source_target_pairs={{0,16},{1,17},{2,18},{3,19},{4,20},{5,21},{6,22},{7,23},{8,24},{9,... | collective-permute-start | bytes 1597448 | tf_op jit(solution)/shard_map/ppermute | solution.py:45
  31.5 28.0 %collective-permute-start.8 = (bf16[1040,256]{1,0:T(8,128)(2,1)S(1)}, bf16[1040,256]{1,0:T(8,128)(2,1)S(1)}, u32[]{:S(2)}, u32[]{:S(2)}) collective-permute-start(bf16[1040,256]{1,0:T(8,128)(2,1)S(1)} %plane.1.refs_0_), channel_id=1, source_target_pairs={{0,32},{1,33},{2,34},{3,35},{4,36},{5,37},{6,38},{7,39},{8,40},{9,... | collective-permute-start | bytes 1597448 | tf_op jit(solution)/shard_map/ppermute | solution.py:45
  34.2 25.3 %collective-permute-start.7 = (bf16[1040,256]{1,0:T(8,128)(2,1)S(1)}, bf16[1040,256]{1,0:T(8,128)(2,1)S(1)}, u32[]{:S(2)}, u32[]{:S(2)}) collective-permute-start(bf16[1040,256]{1,0:T(8,128)(2,1)S(1)} %plane.1.refs_0_), channel_id=1, source_target_pairs={{0,48},{1,49},{2,50},{3,51},{4,52},{5,53},{6,54},{7,55},{8,56},{9,... | collective-permute-start | bytes 1597448 | tf_op jit(solution)/shard_map/ppermute | solution.py:45
  35.6 46.7 %collective-permute-start.10 = (bf16[128,1536]{1,0:T(8,128)(2,1)}, bf16[128,1536]{1,0:T(8,128)(2,1)S(1)}, u32[]{:S(2)}, u32[]{:S(2)}) collective-permute-start(bf16[128,1536]{1,0:T(8,128)(2,1)} %g_own), channel_id=1, source_target_pairs={{0,1},{1,0},{2,3},{3,2},{4,5},{5,4},{6,7},{7,6},{8,9},{9,8},{10,11... | collective-permute-start | bytes 1179656 | tf_op jit(solution)/shard_map/ppermute | solution.py:45
  66.0 18.9 %collective-permute-start.11 = (f32[8,3072]{1,0:T(8,128)S(1)}, f32[8,3072]{1,0:T(8,128)S(1)}, u32[]{:S(2)}, u32[]{:S(2)}) collective-permute-start(f32[8,3072]{1,0:T(8,128)S(1)} %row_statistics.5.mine_ref), channel_id=1, source_target_pairs={{0,1},{1,0},{2,3},{3,2},{4,5},{5,4},{6,7},{7,6},{8,9},{9,8},{10,11... | collective-permute-start | bytes 294920 | tf_op jit(solution)/shard_map/ppermute | solution.py:45
  93.0 16.1 %collective-permute-start.12 = (bf16[1024,256]{1,0:T(8,128)(2,1)S(1)}, bf16[1024,256]{1,0:T(8,128)(2,1)S(1)}, u32[]{:S(2)}, u32[]{:S(2)}) collective-permute-start(bf16[1024,256]{1,0:T(8,128)(2,1)S(1)} %get-tuple-element.78), channel_id=1, source_target_pairs={{0,32},{1,33},{2,34},{3,35},{4,36},{5,37},{6,38},{7,39},{8,40},{9,... | collective-permute-start | bytes 1572872 | tf_op jit(solution)/shard_map/ppermute | solution.py:45
  101.2 15.3 %collective-permute-start.13 = (bf16[1024,256]{1,0:T(8,128)(2,1)S(1)}, bf16[1024,256]{1,0:T(8,128)(2,1)S(1)}, u32[]{:S(2)}, u32[]{:S(2)}) collective-permute-start(bf16[1024,256]{1,0:T(8,128)(2,1)S(1)} %get-tuple-element.87), channel_id=1, source_target_pairs={{0,16},{1,17},{2,18},{3,19},{4,20},{5,21},{6,22},{7,23},{8,24},{9,... | collective-permute-start | bytes 1572872 | tf_op jit(solution)/shard_map/ppermute | solution.py:45
  102.1 14.4 %collective-permute-start.14 = (bf16[1024,256]{1,0:T(8,128)(2,1)S(1)}, bf16[1024,256]{1,0:T(8,128)(2,1)S(1)}, u32[]{:S(2)}, u32[]{:S(2)}) collective-permute-start(bf16[1024,256]{1,0:T(8,128)(2,1)S(1)} %get-tuple-element.88), channel_id=1, source_target_pairs={{0,48},{1,49},{2,50},{3,51},{4,52},{5,53},{6,54},{7,55},{8,56},{9,... | collective-permute-start | bytes 1572872 | tf_op jit(solution)/shard_map/ppermute | solution.py:45
  116.9 14.0 %collective-permute-start.15 = (bf16[256,256]{1,0:T(8,128)(2,1)S(1)}, bf16[256,256]{1,0:T(8,128)(2,1)S(1)}, u32[]{:S(2)}, u32[]{:S(2)}) collective-permute-start(bf16[256,256]{1,0:T(8,128)(2,1)S(1)} %get-tuple-element.100), channel_id=1, source_target_pairs={{0,2},{1,3},{2,4},{3,5},{4,6},{5,7},{6,8},{7,9},{8,10},{9,11},{10,... | collective-permute-start | bytes 393224 | tf_op jit(solution)/shard_map/ppermute | solution.py:45
  126.0 10.1 %collective-permute-start.16 = (bf16[256,256]{1,0:T(8,128)(2,1)S(1)}, bf16[256,256]{1,0:T(8,128)(2,1)S(1)}, u32[]{:S(2)}, u32[]{:S(2)}) collective-permute-start(bf16[256,256]{1,0:T(8,128)(2,1)S(1)} %get-tuple-element.101), channel_id=1, source_target_pairs={{0,14},{1,15},{2,0},{3,1},{4,2},{5,3},{6,4},{7,5},{8,6},{9,7},{10,... | collective-permute-start | bytes 393224 | tf_op jit(solution)/shard_map/ppermute | solution.py:45
  126.7 19.3 %collective-permute-start.20 = (bf16[128,1536]{1,0:T(8,128)(2,1)S(1)}, bf16[128,1536]{1,0:T(8,128)(2,1)S(1)}, u32[]{:S(2)}, u32[]{:S(2)}) collective-permute-start(bf16[128,1536]{1,0:T(8,128)(2,1)S(1)} %get-tuple-element.94), channel_id=1, source_target_pairs={{0,1},{1,0},{2,3},{3,2},{4,5},{5,4},{6,7},{7,6},{8,9},{9,8},{10,11... | collective-permute-start | bytes 1179656 | tf_op jit(solution)/shard_map/ppermute | solution.py:45
  136.3 8.7 %collective-permute-start.17 = (bf16[128,256]{1,0:T(8,128)(2,1)S(1)}, bf16[128,256]{1,0:T(8,128)(2,1)S(1)}, u32[]{:S(2)}, u32[]{:S(2)}) collective-permute-start(bf16[128,256]{1,0:T(8,128)(2,1)S(1)} %get-tuple-element.97), channel_id=1, source_target_pairs={{0,8},{1,9},{2,10},{3,11},{4,12},{5,13},{6,14},{7,15},{8,0},{9,1},... | collective-permute-start | bytes 196616 | tf_op jit(solution)/shard_map/ppermute | solution.py:45
  139.3 6.7 %collective-permute-start.18 = (bf16[128,256]{1,0:T(8,128)(2,1)S(1)}, bf16[128,256]{1,0:T(8,128)(2,1)S(1)}, u32[]{:S(2)}, u32[]{:S(2)}) collective-permute-start(bf16[128,256]{1,0:T(8,128)(2,1)S(1)} %get-tuple-element.98), channel_id=1, source_target_pairs={{0,2},{1,3},{2,4},{3,5},{4,6},{5,7},{6,8},{7,9},{8,10},{9,11},{10,... | collective-permute-start | bytes 196616 | tf_op jit(solution)/shard_map/ppermute | solution.py:45
  139.3 6.7 %collective-permute-start.19 = (bf16[128,256]{1,0:T(8,128)(2,1)S(1)}, bf16[128,256]{1,0:T(8,128)(2,1)S(1)}, u32[]{:S(2)}, u32[]{:S(2)}) collective-permute-start(bf16[128,256]{1,0:T(8,128)(2,1)S(1)} %get-tuple-element.99), channel_id=1, source_target_pairs={{0,14},{1,15},{2,0},{3,1},{4,2},{5,3},{6,4},{7,5},{8,6},{9,7},{10,... | collective-permute-start | bytes 196616 | tf_op jit(solution)/shard_map/ppermute | solution.py:45
  146.1 4.4 %collective-permute-start.21 = (f32[64,256]{1,0:T(8,128)S(1)}, f32[64,256]{1,0:T(8,128)S(1)}, u32[]{:S(2)}, u32[]{:S(2)}) collective-permute-start(f32[64,256]{1,0:T(8,128)S(1)} %get-tuple-element.105), channel_id=1, source_target_pairs={{0,1},{1,0},{2,3},{3,2},{4,5},{5,4},{6,7},{7,6},{8,9},{9,8},{10,11... | collective-permute-start | bytes 196616 | tf_op jit(solution)/shard_map/ppermute | solution.py:45
